TPU v7x, 128 devices: a whole 4x4x4 slice. The times are simulated.
128 devices in a mesh: row: 8 (over y_lo, z), col: 2 (over core), fib: 8 (over y_hi, x).
Axes of the slice: x: 4, y: 4 (y_hi: 2, y_lo: 2; y = y_hi * 2 + y_lo), z: 4, core: 2. Of those that a mesh axis runs over, the one named last changes fastest.
Arguments:
- features: bfloat16 [32768, 1024], P(('row', 'col'), 'fib'), may hold values from -6 to 6
- pre_activation: bfloat16 [32768, 1024], P(('row', 'col'), 'fib'), may hold values from -8 to 8
- out_grad: bfloat16 [32768, 1024], P(('row', 'col'), 'fib'), may hold values from -1.5 to 1.5
- weight: bfloat16 [1024, 1024], P('fib'), may hold values from -0.1875 to 0.1875
- tile_values: bfloat16 [8, 2, 128, 256, 256], P('row', 'col'), may hold values from 0.0019989014 to 0.059814453
- tile_rows: int32 [8, 2, 128], P('row', 'col'), may hold values from 0 to 15, as said below
- tile_cols: int32 [8, 2, 128], P('row', 'col'), may hold values from 0 to 63, as said below
- tile_counts: int32 [8, 2], P('row', 'col'), may hold values from 16 to 128, as said below
Outputs:
- grad_features: bfloat16 [32768, 1024], P(('row', 'col'), 'fib')
- grad_weight: float32 [1024, 1024], P('fib')
Inputs may be any that keep to these rules, and one draw needn't show every extreme that they name: `tile_rows`: within one block the used slots name distinct tiles, rows below 16. `tile_cols`: columns below 64. `tile_counts`: some block uses all 128 slots.
All inputs are finite; a program needn't handle non-finite values.
Results may differ from a plain program's by a relative error of at most 0.0058.
Values may be sent and summed in bfloat16 or wider, within the bound.
A program may use at most 128 MiB of HBM per device.

v0:
```python
import jax
import jax.numpy as jnp
from jax import lax
from jax.sharding import PartitionSpec as P


def split_up(value, dim, peers):
    before, after = (value.shape[:dim], value.shape[dim + 1 :])
    return jnp.moveaxis(value.reshape(*before, peers, -1, *after), dim, 0)


def summed_on_arrival(value, axis, dim):
    peers = lax.axis_size(axis)
    pieces = lax.all_to_all(split_up(value, dim, peers), axis, 0, 0, tiled=True)
    return jnp.sum(pieces, axis=0)


def total_of_pieces(value, axis):
    return lax.all_gather(value, axis).sum(0)


def from_everyone(value, axis):
    peers = lax.axis_size(axis)
    return lax.all_to_all(
        jnp.broadcast_to(value[None], (peers, *value.shape)), axis, 0, 0, tiled=True
    )


def joined_along(pieces, dim):
    dims = list(pieces.shape[1:])
    dims[dim] *= pieces.shape[0]
    return jnp.moveaxis(pieces, 0, dim).reshape(dims)


def gather_directly(value, axis, dim):
    pieces = from_everyone(value, axis)
    return joined_along(pieces, dim)


def place_group(running, products, target, valid, offset):
    out_tiles = running.shape[0]
    local = target - offset
    placing = (
        (local[:, None] == jnp.arange(out_tiles, dtype=jnp.int32)[None, :]) & valid[:, None]
    ).astype(jnp.float32)
    return running + jnp.einsum("st,sif->tif", placing, products, precision=lax.Precision.HIGHEST)


def group_products(tile_block, row_index, col_index, panels_all, first, slot_group, transpose):
    block_vals = lax.dynamic_slice_in_dim(tile_block, first, slot_group, 0)
    block_rows = lax.dynamic_slice_in_dim(row_index, first, slot_group, 0)
    block_cols = lax.dynamic_slice_in_dim(col_index, first, slot_group, 0)
    if transpose:
        products = jnp.einsum(
            "sij,sif->sjf", block_vals, panels_all[block_rows], preferred_element_type=jnp.float32
        )
        return (products, block_cols)
    products = jnp.einsum(
        "sij,sjf->sif", block_vals, panels_all[block_cols], preferred_element_type=jnp.float32
    )
    return (products, block_rows)


def group_total(tile_block, slot_group):
    return tile_block.shape[0] // slot_group


def tile_products(tile_block, row_index, col_index, live_count, panel_source, out_tiles, transpose):
    tile_size = tile_block.shape[1]
    feature_cols = panel_source.shape[1]
    panels_all = panel_source.reshape(-1, tile_size, feature_cols)
    slot_group = 16

    def one_block(block_index, running):
        first = block_index * slot_group
        products, target = group_products(
            tile_block, row_index, col_index, panels_all, first, slot_group, transpose
        )
        valid = first + jnp.arange(slot_group, dtype=jnp.int32) < live_count
        return place_group(running, products, target, valid, 0)

    initial = jnp.zeros((out_tiles, tile_size, feature_cols), jnp.float32)
    running = lax.fori_loop(0, group_total(tile_block, slot_group), one_block, initial)
    return running.reshape(out_tiles * tile_size, feature_cols)


def on_device(
    features, pre_activation, out_grad, weight, tile_values, tile_rows, tile_cols, tile_counts
):
    tile_block = tile_values[0, 0]
    row_index = tile_rows[0, 0]
    col_index = tile_cols[0, 0]
    live_count = tile_counts[0, 0]
    node_dev = features.shape[0]
    tile_size = tile_block.shape[1]
    row_tiles = node_dev * lax.axis_size("col") // tile_size
    col_tiles = node_dev * lax.axis_size("row") // tile_size
    column_block = lax.all_gather(features, "row", axis=0, tiled=True)
    partial_value = tile_products(
        tile_block, row_index, col_index, live_count, column_block, row_tiles, False
    )
    aggregated = summed_on_arrival(partial_value, "col", 0).astype(jnp.bfloat16)
    pre_value = pre_activation.astype(jnp.float32)
    sigmoid_value = jax.nn.sigmoid(pre_value)
    grad_local = (
        out_grad.astype(jnp.float32) * sigmoid_value * (1.0 + pre_value * (1.0 - sigmoid_value))
    ).astype(jnp.bfloat16)
    full_grad = lax.all_gather(grad_local, "fib", axis=1, tiled=True)
    weight_part = lax.dot_general(
        aggregated, full_grad, (((0,), (0,)), ((), ())), preferred_element_type=jnp.float32
    )
    grad_weight = total_of_pieces(weight_part, ("row", "col"))
    projected = lax.dot_general(
        full_grad, weight, (((1,), (1,)), ((), ())), preferred_element_type=jnp.float32
    ).astype(jnp.bfloat16)
    row_block = gather_directly(projected, "col", 0)
    transposed = tile_products(
        tile_block, row_index, col_index, live_count, row_block, col_tiles, True
    )
    grad_features = lax.psum_scatter(transposed, "row", scatter_dimension=0, tiled=True).astype(
        jnp.bfloat16
    )
    return (grad_features, grad_weight)


def solution(mesh):
    in_specs = (
        P(("row", "col"), "fib"),
        P(("row", "col"), "fib"),
        P(("row", "col"), "fib"),
        P("fib", None),
        P("row", "col", None, None, None),
        P("row", "col", None),
        P("row", "col", None),
        P("row", "col"),
    )
    out_specs = (P(("row", "col"), "fib"), P("fib", None))
    return jax.shard_map(
        on_device, mesh=mesh, in_specs=in_specs, out_specs=out_specs, check_vma=False
    )
```

profile of v0, /device:TPU:1, one launch (start us, length us, event | category | flops | bytes accessed | tf_op | source)
XLA Modules:
  0.0 379.1 jit_solution(10993640622262767804)
XLA Ops:
  10.5 55.2 %all-gather.7.cloned.1.call-done = bf16[16384,128]{1,0:T(8,128)(2,1)} async-done(((bf16[2048,128]{1,0:T(8,128)(2,1)}), bf16[16384,128]{1,0:T(8,128)(2,1)}) %all-gather.7.cloned.1.call-update) | async-done | bytes 4194320 | tf_op jit(solution)/shard_map/all_gather | solution.py:98
  65.7 76.0 %while.29 = (s32[]{:T(128)}, f32[16,256,128]{2,0,1:T(8,128)S(1)}, s32[128]{0:T(128)S(1)}, s32[]{:T(128)}, bf16[128,256,256]{2,1,0:T(8,128)(2,1)}, /*index=5*/s32...) while((s32[]{:T(128)}, f32[16,256,128]{2,0,1:T(8,128)S(1)}, ...), condition=%wide.region_4.0_spmd.clone, body=%wide.region_3.0_spmd.clone.sunk | while | flops 370148960 | bytes 13636257 | solution.py:83
  66.6 2.9 gather_fusion.1
  71.8 3.4 select_add_fusion.5
  76.0 3.2 gather_fusion.1
  81.5 3.4 select_add_fusion.5
  85.7 2.9 gather_fusion.1
  91.0 3.4 select_add_fusion.5
  95.2 2.9 gather_fusion.1
  100.5 3.4 select_add_fusion.5
  104.7 3.0 gather_fusion.1
  110.0 3.4 select_add_fusion.5
  119.5 3.4 select_add_fusion.5
  123.7 2.9 gather_fusion.1
  128.9 3.4 select_add_fusion.5
  138.4 3.4 select_add_fusion.5
  142.4 5.7 %all_to_all.10 = f32[2,2048,128]{2,1,0:T(8,128)S(1)} all-to-all(f32[2,2048,128]{2,1,0:T(8,128)S(1)} %bitcast.33), channel_id=1, replica_groups=mesh['row'=8,'col'=2,'fib'=8] {'col'}, dimensions={0} | all-to-all | bytes 4194304 | tf_op jit(solution)/shard_map/all_to_all | solution.py:14
  148.2 3.7 fusion.29
  152.1 3.4 convolution_convert_fusion
  155.6 4.7 %all_to_all.11 = bf16[2,2048,128]{2,1,0:T(8,128)(2,1)S(1)} all-to-all(bf16[2,2048,128]{2,1,0:T(8,128)(2,1)S(1)} %broadcast_in_dim.45), channel_id=1, replica_groups=mesh['row'=8,'col'=2,'fib'=8] {'col'}, dimensions={0} | all-to-all | bytes 2097152 | tf_op jit(solution)/shard_map/all_to_all | solution.py:24
  160.3 106.9 %while.28 = (s32[]{:T(128)}, f32[64,256,128]{2,0,1:T(8,128)}, s32[128]{0:T(128)S(1)}, s32[]{:T(128)}, bf16[128,256,256]{2,1,0:T(8,128)(2,1)}, /*index=5*/s32[128...) while((s32[]{:T(128)}, f32[64,256,128]{2,0,1:T(8,128)}, ...), condition=%wide.region_1.0_spmd.clone, body=%wide.region_0.0_spmd.clone.sunk | while | flops 675286144 | bytes 26219168 | solution.py:83
  164.2 7.5 %select_add_fusion.4 = f32[64,256,128]{2,0,1:T(8,128)} fusion(f32[64,256,128]{2,0,1:T(8,128)} %get-tuple-element.426, pred[]{:T(512)S(6)} %compare.6, f32[16,256,128]{2,1,0:T(8,128)S(1)} %fusion.50, s32[16]{0:T(128)S(1)} %dynamic_slice.62, pred[16]{0:T(512)(128)(4,1)S(1)} %add_compare_fusion.4), kind=kOutput, calls=%fused_computation.2.clone.1 | convolution fusion | flops 406849536 | bytes 18874448 | tf_op jit(solution)/shard_map/while/body/eval_jaxpr/st,sif->tif/dot_general | solution.py:46
  175.8 9.7 %select_add_fusion.4 = f32[64,256,128]{2,0,1:T(8,128)} fusion(f32[64,256,128]{2,0,1:T(8,128)} %get-tuple-element.426, pred[]{:T(512)S(6)} %compare.6, f32[16,256,128]{2,1,0:T(8,128)S(1)} %fusion.50, s32[16]{0:T(128)S(1)} %dynamic_slice.62, pred[16]{0:T(512)(128)(4,1)S(1)} %add_compare_fusion.4), kind=kOutput, calls=%fused_computation.2.clone.1 | convolution fusion | flops 406849536 | bytes 18874448 | tf_op jit(solution)/shard_map/while/body/eval_jaxpr/st,sif->tif/dot_general | solution.py:46
  189.5 9.7 %select_add_fusion.4 = f32[64,256,128]{2,0,1:T(8,128)} fusion(f32[64,256,128]{2,0,1:T(8,128)} %get-tuple-element.426, pred[]{:T(512)S(6)} %compare.6, f32[16,256,128]{2,1,0:T(8,128)S(1)} %fusion.50, s32[16]{0:T(128)S(1)} %dynamic_slice.62, pred[16]{0:T(512)(128)(4,1)S(1)} %add_compare_fusion.4), kind=kOutput, calls=%fused_computation.2.clone.1 | convolution fusion | flops 406849536 | bytes 18874448 | tf_op jit(solution)/shard_map/while/body/eval_jaxpr/st,sif->tif/dot_general | solution.py:46
  203.2 9.7 %select_add_fusion.4 = f32[64,256,128]{2,0,1:T(8,128)} fusion(f32[64,256,128]{2,0,1:T(8,128)} %get-tuple-element.426, pred[]{:T(512)S(6)} %compare.6, f32[16,256,128]{2,1,0:T(8,128)S(1)} %fusion.50, s32[16]{0:T(128)S(1)} %dynamic_slice.62, pred[16]{0:T(512)(128)(4,1)S(1)} %add_compare_fusion.4), kind=kOutput, calls=%fused_computation.2.clone.1 | convolution fusion | flops 406849536 | bytes 18874448 | tf_op jit(solution)/shard_map/while/body/eval_jaxpr/st,sif->tif/dot_general | solution.py:46
  216.8 9.7 %select_add_fusion.4 = f32[64,256,128]{2,0,1:T(8,128)} fusion(f32[64,256,128]{2,0,1:T(8,128)} %get-tuple-element.426, pred[]{:T(512)S(6)} %compare.6, f32[16,256,128]{2,1,0:T(8,128)S(1)} %fusion.50, s32[16]{0:T(128)S(1)} %dynamic_slice.62, pred[16]{0:T(512)(128)(4,1)S(1)} %add_compare_fusion.4), kind=kOutput, calls=%fused_computation.2.clone.1 | convolution fusion | flops 406849536 | bytes 18874448 | tf_op jit(solution)/shard_map/while/body/eval_jaxpr/st,sif->tif/dot_general | solution.py:46
  230.4 9.7 %select_add_fusion.4 = f32[64,256,128]{2,0,1:T(8,128)} fusion(f32[64,256,128]{2,0,1:T(8,128)} %get-tuple-element.426, pred[]{:T(512)S(6)} %compare.6, f32[16,256,128]{2,1,0:T(8,128)S(1)} %fusion.50, s32[16]{0:T(128)S(1)} %dynamic_slice.62, pred[16]{0:T(512)(128)(4,1)S(1)} %add_compare_fusion.4), kind=kOutput, calls=%fused_computation.2.clone.1 | convolution fusion | flops 406849536 | bytes 18874448 | tf_op jit(solution)/shard_map/while/body/eval_jaxpr/st,sif->tif/dot_general | solution.py:46
  244.0 9.7 %select_add_fusion.4 = f32[64,256,128]{2,0,1:T(8,128)} fusion(f32[64,256,128]{2,0,1:T(8,128)} %get-tuple-element.426, pred[]{:T(512)S(6)} %compare.6, f32[16,256,128]{2,1,0:T(8,128)S(1)} %fusion.50, s32[16]{0:T(128)S(1)} %dynamic_slice.62, pred[16]{0:T(512)(128)(4,1)S(1)} %add_compare_fusion.4), kind=kOutput, calls=%fused_computation.2.clone.1 | convolution fusion | flops 406849536 | bytes 18874448 | tf_op jit(solution)/shard_map/while/body/eval_jaxpr/st,sif->tif/dot_general | solution.py:46
  257.6 9.7 %select_add_fusion.4 = f32[64,256,128]{2,0,1:T(8,128)} fusion(f32[64,256,128]{2,0,1:T(8,128)} %get-tuple-element.426, pred[]{:T(512)S(6)} %compare.6, f32[16,256,128]{2,1,0:T(8,128)S(1)} %fusion.50, s32[16]{0:T(128)S(1)} %dynamic_slice.62, pred[16]{0:T(512)(128)(4,1)S(1)} %add_compare_fusion.4), kind=kOutput, calls=%fused_computation.2.clone.1 | convolution fusion | flops 406849536 | bytes 18874448 | tf_op jit(solution)/shard_map/while/body/eval_jaxpr/st,sif->tif/dot_general | solution.py:46
  267.2 11.5 %copy.11 = f32[64,256,128]{2,1,0:T(8,128)} copy(f32[64,256,128]{2,0,1:T(8,128)} %get-tuple-element.250) | data formatting | bytes 16777216 | tf_op jit(solution)/shard_map/while | solution.py:83
  278.8 5.1 %reduce_sum.19 = f32[128,1024]{1,0:T(8,128)} reduce(f32[16,128,1024]{2,1,0:T(8,128)} %bitcast.32, f32[]{:T(128)} %constant.71.clone.1), dimensions={0}, to_apply=%region_6.0 | reduce | flops 1966080 | bytes 8912900 | tf_op jit(solution)/shard_map/reduce_sum | solution.py:19
  283.8 86.7 %reduce-scatter.2.cloned.1.call-done = f32[2048,128]{1,0:T(8,128)} async-done(((f32[16384,128]{1,0:T(8,128)}), f32[2048,128]{1,0:T(8,128)}) %reduce-scatter.2.cloned.1.call-update) | async-done | bytes 1048592 | tf_op jit(solution)/shard_map/reduce_scatter | solution.py:120
  (115 shorter events, 68.5 us)
Async XLA Ops:
  7.2 144.9 %copy-start = (bf16[128,1024]{1,0:T(8,128)(2,1)S(1)}, bf16[128,1024]{1,0:T(8,128)(2,1)}, u32[]{:S(2)}) copy-start(bf16[128,1024]{1,0:T(8,128)(2,1)} %param.15) | copy-start | bytes 786436
  7.2 58.6 %copy-start.3 = (s32[1,1,128]{2,1,0:T(1,128)S(1)}, s32[1,1,128]{2,1,0:T(1,128)}, u32[]{:S(2)}) copy-start(s32[1,1,128]{2,1,0:T(1,128)} %param.18) | copy-start | bytes 1540
  7.2 58.6 %copy-start.2 = (s32[1,1,128]{2,1,0:T(1,128)S(1)}, s32[1,1,128]{2,1,0:T(1,128)}, u32[]{:S(2)}) copy-start(s32[1,1,128]{2,1,0:T(1,128)} %param.17) | copy-start | bytes 1540
  7.2 58.5 %all-gather.7.cloned.1.call-start = ((), (), s32[]{:S(2)}) async-start(), calls=%async_computation.5 | async-start | bytes 4718592 | tf_op jit(solution)/shard_map/all_gather | solution.py:98
  7.9 140.3 %all-gather.5.cloned.1.call-start = ((), (), s32[]{:S(2)}) async-start(), calls=%async_computation.3 | async-start | bytes 4718592 | tf_op jit(solution)/shard_map/all_gather | solution.py:108
  10.4 268.3 %all-gather.9.cloned.1.call-start = ((), (), s32[]{:S(2)}) async-start(), calls=%async_computation.6 | async-start | bytes 8912896 | tf_op jit(solution)/shard_map/all_gather | solution.py:19
  152.0 218.5 %reduce-scatter.2.cloned.1.call-start = ((), (), s32[]{:S(2)}) async-start(), calls=%async_computation.4 | async-start | bytes 9437184 | tf_op jit(solution)/shard_map/reduce_scatter | solution.py:120
  278.7 93.8 %copy-start.1 = (bf16[128,1024]{1,0:T(8,128)(2,1)S(1)}, bf16[128,1024]{1,0:T(8,128)(2,1)}, u32[]{:S(2)}) copy-start(bf16[128,1024]{1,0:T(8,128)(2,1)} %param.15) | copy-start | bytes 786436
Sparse Core Ops, SparseCore 0:
  9.7 56.0 all-gather.6
  68.5 75.8 all-gather.4
  152.1 50.9 all-gather.8
  278.8 91.6 reduce-scatter.1
where the time goes:
time: 380 us; the launch traced here: 379 us
  matrix products  147 us (39%)
  waiting for transfers between devices  143 us (38%)
  local copies, waits for them, and re-layouts  43.3 us (11%)
  other arithmetic  21.5 us (6%)
  between operations  13.9 us (4%)
  blocking collectives  10.4 us (3%)
    dot_general x16, matrix products, place_group(): jnp.einsum('st,sif->tif', placing, products, precision=lax.Precision.HIGH...  102 us
    reduce_scatter x1, waiting for transfers between devices, on_device(): lax.psum_scatter(transposed, 'row', scatter_dimension=0, tiled=True)  86.7 us
    all_gather x1, waiting for transfers between devices, on_device(): column_block = lax.all_gather(features, 'row', axis=0, tiled=True)  55.2 us
    gather x8, local copies, waits for them, and re-layouts, group_products(): panels_all[block_cols]  23.9 us
    dot_general x8, matrix products, group_products(): jnp.einsum('sij,sif->sjf', block_vals, panels_all[block_rows], preferred_...  19 us
    dot_general x8, matrix products, group_products(): jnp.einsum('sij,sjf->sif', block_vals, panels_all[block_cols], preferred_...  18.4 us
    while x2, local copies, waits for them, and re-layouts, tile_products(): lax.fori_loop(0, group_total(tile_block, slot_group), one_block, initial)  12.1 us
    lt x16, other arithmetic, one_block(): valid = first + jnp.arange(slot_group, dtype=jnp.int32) < live_count  10.4 us
  transfers between devices with their start and end apart: 4, of which 2 were waited for; matrix products, arithmetic and copies ran while one was open for 54% of the time, Pallas kernels for 0%

commit v1 on v0

--- a/solution.py
+++ b/solution.py
@@ -95,7 +95,9 @@
     tile_size = tile_block.shape[1]
     row_tiles = node_dev * lax.axis_size("col") // tile_size
     col_tiles = node_dev * lax.axis_size("row") // tile_size
-    column_block = lax.all_gather(features, "row", axis=0, tiled=True)
+    column_block = jnp.concatenate(
+        lax.all_to_all(jnp.stack([features] * lax.axis_size("row")), "row", 0, 0), axis=0
+    )
     partial_value = tile_products(
         tile_block, row_index, col_index, live_count, column_block, row_tiles, False
     )

time: 380 us -> 396 us (1.042)
  starting transfers between devices: 0.16 us -> 7.13 us
    all_to_all x0 -> x1, waiting for transfers between devices: none -> 56.3 us  [on_device(): lax.all_to_all(jnp.stack([features] * lax.axis_size('row')), 'row', 0, 0)]
    all_gather x1 -> x0, waiting for transfers between devices: 55.2 us -> none  [on_device(): column_block = lax.all_gather(features, 'row', axis=0, tiled=True)]
    all_to_all x0 -> x1, starting transfers between devices: none -> 7.01 us  [on_device(): lax.all_to_all(jnp.stack([features] * lax.axis_size('row')), 'row', 0, 0)]
  transfers between devices with their start and end apart: 4 -> 4, of which waited for: 2 -> 2; matrix products, arithmetic and copies ran while one was open for 54% -> 52% of each run, Pallas kernels for 0% -> 0%
where the time goes in v1:
time: 396 us; the launch traced here: 395 us
  matrix products  147 us (37%)
  waiting for transfers between devices  145 us (37%)
  local copies, waits for them, and re-layouts  46.6 us (12%)
  other arithmetic  20.3 us (5%)
  blocking collectives  14.2 us (4%)
  between operations  13.9 us (4%)
  starting transfers between devices  7.13 us (2%)
    dot_general x16, matrix products, place_group(): jnp.einsum('st,sif->tif', placing, products, precision=lax.Precision.HIGH...  102 us
    reduce_scatter x1, waiting for transfers between devices, on_device(): lax.psum_scatter(transposed, 'row', scatter_dimension=0, tiled=True)  89 us
    all_to_all x1, waiting for transfers between devices, on_device(): lax.all_to_all(jnp.stack([features] * lax.axis_size('row')), 'row', 0, 0)  56.3 us
    gather x8, local copies, waits for them, and re-layouts, group_products(): panels_all[block_cols]  23.6 us
    dot_general x8, matrix products, group_products(): jnp.einsum('sij,sif->sjf', block_vals, panels_all[block_rows], preferred_...  19.1 us
    dot_general x8, matrix products, group_products(): jnp.einsum('sij,sjf->sif', block_vals, panels_all[block_cols], preferred_...  18.3 us
    while x2, local copies, waits for them, and re-layouts, tile_products(): lax.fori_loop(0, group_total(tile_block, slot_group), one_block, initial)  12.2 us
    lt x16, other arithmetic, one_block(): valid = first + jnp.arange(slot_group, dtype=jnp.int32) < live_count  10.4 us
  transfers between devices with their start and end apart: 4, of which 2 were waited for; matrix products, arithmetic and copies ran while one was open for 52% of the time, Pallas kernels for 0%

profile of v1, /device:TPU:1, one launch (start us, length us, event | category | flops | bytes accessed | tf_op | source)
XLA Modules:
  0.0 394.8 jit_solution(16182339428216935280)
XLA Ops:
  7.2 3.6 stack.2
  10.8 7.0 %all-to-all-start.1 = ((bf16[8,2048,128]{2,1,0:T(8,128)(2,1)}), bf16[8,2048,128]{2,1,0:T(8,128)(2,1)}, u32[]{:S(2)}, u32[]{:S(2)}) async-start(bf16[8,2048,128]{2,1,0:T(8,128)(2,1)} %stack.2), calls=%async_computation.2 | async-start | bytes 8388608 | tf_op jit(solution)/shard_map/all_to_all | solution.py:99
  19.2 56.3 %all-to-all-done.1 = bf16[8,2048,128]{2,1,0:T(8,128)(2,1)} async-done(((bf16[8,2048,128]{2,1,0:T(8,128)(2,1)}), bf16[8,2048,128]{2,1,0:T(8,128)(2,1)}, u32[]{:S(2)}, u32[]{:S(2)}) %all-to-all-start.1) | async-done | bytes 4194336 | tf_op jit(solution)/shard_map/all_to_all | solution.py:99
  75.4 75.7 %while.29 = (s32[]{:T(128)}, f32[16,256,128]{2,0,1:T(8,128)S(1)}, s32[128]{0:T(128)S(1)}, s32[]{:T(128)}, bf16[128,256,256]{2,1,0:T(8,128)(2,1)}, /*index=5*/s32...) while((s32[]{:T(128)}, f32[16,256,128]{2,0,1:T(8,128)S(1)}, ...), condition=%wide.region_4.0_spmd.clone, body=%wide.region_3.0_spmd.clone.sunk | while | flops 370148960 | bytes 13636257 | solution.py:83
  81.5 3.4 select_add_fusion.5
  85.7 2.9 gather_fusion.1
  90.9 3.4 select_add_fusion.5
  95.2 3.0 gather_fusion.1
  100.5 3.4 select_add_fusion.5
  104.7 3.0 gather_fusion.1
  110.0 3.4 select_add_fusion.5
  114.2 2.9 gather_fusion.1
  119.4 3.4 select_add_fusion.5
  128.9 3.4 select_add_fusion.5
  138.3 3.4 select_add_fusion.5
  147.8 3.4 select_add_fusion.5
  151.8 9.6 %all_to_all.15 = f32[2,2048,128]{2,1,0:T(8,128)S(1)} all-to-all(f32[2,2048,128]{2,1,0:T(8,128)S(1)} %bitcast.33), channel_id=1, replica_groups=mesh['row'=8,'col'=2,'fib'=8] {'col'}, dimensions={0} | all-to-all | bytes 4194304 | tf_op jit(solution)/shard_map/all_to_all | solution.py:14
  161.6 3.7 fusion.29
  165.4 3.4 convolution_convert_fusion
  168.9 4.6 %all_to_all.16 = bf16[2,2048,128]{2,1,0:T(8,128)(2,1)S(1)} all-to-all(bf16[2,2048,128]{2,1,0:T(8,128)(2,1)S(1)} %broadcast_in_dim.45), channel_id=1, replica_groups=mesh['row'=8,'col'=2,'fib'=8] {'col'}, dimensions={0} | all-to-all | bytes 2097152 | tf_op jit(solution)/shard_map/all_to_all | solution.py:24
  173.6 107.1 %while.28 = (s32[]{:T(128)}, f32[64,256,128]{2,0,1:T(8,128)}, s32[128]{0:T(128)S(1)}, s32[]{:T(128)}, bf16[128,256,256]{2,1,0:T(8,128)(2,1)}, /*index=5*/s32[128...) while((s32[]{:T(128)}, f32[64,256,128]{2,0,1:T(8,128)}, ...), condition=%wide.region_1.0_spmd.clone, body=%wide.region_0.0_spmd.clone.sunk | while | flops 675286144 | bytes 26219168 | solution.py:83
  177.7 7.5 %select_add_fusion.4 = f32[64,256,128]{2,0,1:T(8,128)} fusion(f32[64,256,128]{2,0,1:T(8,128)} %get-tuple-element.426, pred[]{:T(512)S(6)} %compare.6, f32[16,256,128]{2,1,0:T(8,128)S(1)} %fusion.50, s32[16]{0:T(128)S(1)} %dynamic_slice.62, pred[16]{0:T(512)(128)(4,1)S(1)} %add_compare_fusion.4), kind=kOutput, calls=%fused_computation.2.clone.1 | convolution fusion | flops 406849536 | bytes 18874448 | tf_op jit(solution)/shard_map/while/body/eval_jaxpr/st,sif->tif/dot_general | solution.py:46
  189.1 9.7 %select_add_fusion.4 = f32[64,256,128]{2,0,1:T(8,128)} fusion(f32[64,256,128]{2,0,1:T(8,128)} %get-tuple-element.426, pred[]{:T(512)S(6)} %compare.6, f32[16,256,128]{2,1,0:T(8,128)S(1)} %fusion.50, s32[16]{0:T(128)S(1)} %dynamic_slice.62, pred[16]{0:T(512)(128)(4,1)S(1)} %add_compare_fusion.4), kind=kOutput, calls=%fused_computation.2.clone.1 | convolution fusion | flops 406849536 | bytes 18874448 | tf_op jit(solution)/shard_map/while/body/eval_jaxpr/st,sif->tif/dot_general | solution.py:46
  202.8 9.7 %select_add_fusion.4 = f32[64,256,128]{2,0,1:T(8,128)} fusion(f32[64,256,128]{2,0,1:T(8,128)} %get-tuple-element.426, pred[]{:T(512)S(6)} %compare.6, f32[16,256,128]{2,1,0:T(8,128)S(1)} %fusion.50, s32[16]{0:T(128)S(1)} %dynamic_slice.62, pred[16]{0:T(512)(128)(4,1)S(1)} %add_compare_fusion.4), kind=kOutput, calls=%fused_computation.2.clone.1 | convolution fusion | flops 406849536 | bytes 18874448 | tf_op jit(solution)/shard_map/while/body/eval_jaxpr/st,sif->tif/dot_general | solution.py:46
  216.6 9.7 %select_add_fusion.4 = f32[64,256,128]{2,0,1:T(8,128)} fusion(f32[64,256,128]{2,0,1:T(8,128)} %get-tuple-element.426, pred[]{:T(512)S(6)} %compare.6, f32[16,256,128]{2,1,0:T(8,128)S(1)} %fusion.50, s32[16]{0:T(128)S(1)} %dynamic_slice.62, pred[16]{0:T(512)(128)(4,1)S(1)} %add_compare_fusion.4), kind=kOutput, calls=%fused_computation.2.clone.1 | convolution fusion | flops 406849536 | bytes 18874448 | tf_op jit(solution)/shard_map/while/body/eval_jaxpr/st,sif->tif/dot_general | solution.py:46
  230.2 9.7 %select_add_fusion.4 = f32[64,256,128]{2,0,1:T(8,128)} fusion(f32[64,256,128]{2,0,1:T(8,128)} %get-tuple-element.426, pred[]{:T(512)S(6)} %compare.6, f32[16,256,128]{2,1,0:T(8,128)S(1)} %fusion.50, s32[16]{0:T(128)S(1)} %dynamic_slice.62, pred[16]{0:T(512)(128)(4,1)S(1)} %add_compare_fusion.4), kind=kOutput, calls=%fused_computation.2.clone.1 | convolution fusion | flops 406849536 | bytes 18874448 | tf_op jit(solution)/shard_map/while/body/eval_jaxpr/st,sif->tif/dot_general | solution.py:46
  243.8 9.7 %select_add_fusion.4 = f32[64,256,128]{2,0,1:T(8,128)} fusion(f32[64,256,128]{2,0,1:T(8,128)} %get-tuple-element.426, pred[]{:T(512)S(6)} %compare.6, f32[16,256,128]{2,1,0:T(8,128)S(1)} %fusion.50, s32[16]{0:T(128)S(1)} %dynamic_slice.62, pred[16]{0:T(512)(128)(4,1)S(1)} %add_compare_fusion.4), kind=kOutput, calls=%fused_computation.2.clone.1 | convolution fusion | flops 406849536 | bytes 18874448 | tf_op jit(solution)/shard_map/while/body/eval_jaxpr/st,sif->tif/dot_general | solution.py:46
  257.4 9.7 %select_add_fusion.4 = f32[64,256,128]{2,0,1:T(8,128)} fusion(f32[64,256,128]{2,0,1:T(8,128)} %get-tuple-element.426, pred[]{:T(512)S(6)} %compare.6, f32[16,256,128]{2,1,0:T(8,128)S(1)} %fusion.50, s32[16]{0:T(128)S(1)} %dynamic_slice.62, pred[16]{0:T(512)(128)(4,1)S(1)} %add_compare_fusion.4), kind=kOutput, calls=%fused_computation.2.clone.1 | convolution fusion | flops 406849536 | bytes 18874448 | tf_op jit(solution)/shard_map/while/body/eval_jaxpr/st,sif->tif/dot_general | solution.py:46
  271.0 9.7 %select_add_fusion.4 = f32[64,256,128]{2,0,1:T(8,128)} fusion(f32[64,256,128]{2,0,1:T(8,128)} %get-tuple-element.426, pred[]{:T(512)S(6)} %compare.6, f32[16,256,128]{2,1,0:T(8,128)S(1)} %fusion.50, s32[16]{0:T(128)S(1)} %dynamic_slice.62, pred[16]{0:T(512)(128)(4,1)S(1)} %add_compare_fusion.4), kind=kOutput, calls=%fused_computation.2.clone.1 | convolution fusion | flops 406849536 | bytes 18874448 | tf_op jit(solution)/shard_map/while/body/eval_jaxpr/st,sif->tif/dot_general | solution.py:46
  280.6 11.5 %copy.11 = f32[64,256,128]{2,1,0:T(8,128)} copy(f32[64,256,128]{2,0,1:T(8,128)} %get-tuple-element.250) | data formatting | bytes 16777216 | tf_op jit(solution)/shard_map/while | solution.py:83
  292.2 5.1 %reduce_sum.19 = f32[128,1024]{1,0:T(8,128)} reduce(f32[16,128,1024]{2,1,0:T(8,128)} %bitcast.32, f32[]{:T(128)} %constant.71.clone.1), dimensions={0}, to_apply=%region_6.0 | reduce | flops 1966080 | bytes 8912900 | tf_op jit(solution)/shard_map/reduce_sum | solution.py:19
  297.2 89.0 %reduce-scatter.2.cloned.1.call-done = f32[2048,128]{1,0:T(8,128)} async-done(((f32[16384,128]{1,0:T(8,128)}), f32[2048,128]{1,0:T(8,128)}) %reduce-scatter.2.cloned.1.call-update) | async-done | bytes 1048592 | tf_op jit(solution)/shard_map/reduce_scatter | solution.py:122
  (119 shorter events, 72.6 us)
Async XLA Ops:
  7.2 158.2 %copy-start = (bf16[128,1024]{1,0:T(8,128)(2,1)S(1)}, bf16[128,1024]{1,0:T(8,128)(2,1)}, u32[]{:S(2)}) copy-start(bf16[128,1024]{1,0:T(8,128)(2,1)} %param.15) | copy-start | bytes 786436
  10.8 7.1 %copy-start.2 = (bf16[2048,128]{1,0:T(8,128)(2,1)S(1)}, bf16[2048,128]{1,0:T(8,128)(2,1)}, u32[]{:S(2)}) copy-start(bf16[2048,128]{1,0:T(8,128)(2,1)} %param.13) | copy-start | bytes 1572868
  10.8 7.1 %copy-start.3 = (bf16[2048,128]{1,0:T(8,128)(2,1)S(1)}, bf16[2048,128]{1,0:T(8,128)(2,1)}, u32[]{:S(2)}) copy-start(bf16[2048,128]{1,0:T(8,128)(2,1)} %param.14) | copy-start | bytes 1572868
  10.8 64.7 %all-to-all-start.1 = ((bf16[8,2048,128]{2,1,0:T(8,128)(2,1)}), bf16[8,2048,128]{2,1,0:T(8,128)(2,1)}, u32[]{:S(2)}, u32[]{:S(2)}) async-start(bf16[8,2048,128]{2,1,0:T(8,128)(2,1)} %stack.2), calls=%async_computation.2 | async-start | bytes 8388608 | tf_op jit(solution)/shard_map/all_to_all | solution.py:99
  17.8 57.7 %copy-start.4 = (s32[1,1,128]{2,1,0:T(1,128)S(1)}, s32[1,1,128]{2,1,0:T(1,128)}, u32[]{:S(2)}) copy-start(s32[1,1,128]{2,1,0:T(1,128)} %param.17) | copy-start | bytes 1540
  17.8 57.6 %copy-start.5 = (s32[1,1,128]{2,1,0:T(1,128)S(1)}, s32[1,1,128]{2,1,0:T(1,128)}, u32[]{:S(2)}) copy-start(s32[1,1,128]{2,1,0:T(1,128)} %param.18) | copy-start | bytes 1540
  17.8 143.8 %all-gather.4.cloned.1.call-start = ((), (), s32[]{:S(2)}) async-start(), calls=%async_computation.4 | async-start | bytes 4718592 | tf_op jit(solution)/shard_map/all_gather | solution.py:110
  19.1 273.0 %all-gather.6.cloned.1.call-start = ((), (), s32[]{:S(2)}) async-start(), calls=%async_computation.6 | async-start | bytes 8912896 | tf_op jit(solution)/shard_map/all_gather | solution.py:19
  165.3 220.9 %reduce-scatter.2.cloned.1.call-start = ((), (), s32[]{:S(2)}) async-start(), calls=%async_computation.5 | async-start | bytes 9437184 | tf_op jit(solution)/shard_map/reduce_scatter | solution.py:122
  292.2 96.1 %copy-start.1 = (bf16[128,1024]{1,0:T(8,128)(2,1)S(1)}, bf16[128,1024]{1,0:T(8,128)(2,1)}, u32[]{:S(2)}) copy-start(bf16[128,1024]{1,0:T(8,128)(2,1)} %param.15) | copy-start | bytes 786436
Sparse Core Ops, SparseCore 0:
  21.4 90.0 all-gather.3
  165.5 53.3 all-gather.5
  292.2 93.9 reduce-scatter.1
